TPU v7x, 256 devices: a whole 4x4x8 slice. The times are simulated.
256 devices in a mesh: replica: 4 (over y), fsdp: 32 (over x, z), tensor: 2 (over core).
Axes of the slice: x: 4, y: 4, z: 8, core: 2. Of those that a mesh axis runs over, the one named last changes fastest.
Arguments:
- weight: bfloat16 [14336, 4096], P('fsdp', 'tensor'), may hold values from -0.046875 to 0.046875
- momentum: float32 [4, 14336, 4096], P('replica', 'fsdp', 'tensor'), may hold values from -6 to 6
- grad: bfloat16 [4, 14336, 4096], P('replica', 'fsdp', 'tensor'), may hold values from -270 to 270
- basis: float32 [4096, 256], P('tensor', 'fsdp'), may hold values from -0.09375 to 0.09375
Outputs:
- new_weight: bfloat16 [14336, 4096], P('fsdp', 'tensor')
- new_momentum: float32 [4, 14336, 4096], P('replica', 'fsdp', 'tensor')
- new_basis: float32 [4096, 256], P('tensor', 'fsdp')
All inputs are finite; a program needn't handle non-finite values.
Results may differ from a plain program's by a relative error of at most 0.001.
Values sent between devices are 32-bit elements; how exact they have to be, the bound alone decides.
A program may use at most 64 MiB of HBM per device.

v0:
```python
import math

import jax
import jax.numpy as jnp
from jax import lax
from jax.sharding import PartitionSpec as P

ROWS = 14336
COLS = 4096


def product(first, second):
    return jnp.dot(first, second, precision=lax.Precision.HIGHEST)


def solve_right(lower_factor, values):
    return lax.linalg.triangular_solve(
        lower_factor, values, left_side=False, lower=True, transpose_a=True
    )


def normalize_full(right_factor):
    squares = lax.psum(jnp.sum(right_factor * right_factor, axis=0, keepdims=True), "tensor")
    return right_factor / jnp.sqrt(squares + 1e-06)


def body(weight, momentum, grad, basis):
    replicas = lax.axis_size("replica")
    buffer = momentum + grad.astype(jnp.float32)
    owned = buffer[0]
    partial_left = product(owned, lax.all_gather(basis, "fsdp", axis=1, tiled=True))
    left_factor = lax.psum(partial_left, ("replica", "tensor")) / replicas
    gram_matrix = lax.psum(product(left_factor.T, left_factor), "fsdp")
    lower_factor = jnp.linalg.cholesky(gram_matrix)
    ortho_factor = solve_right(lower_factor, left_factor)
    trans_part = product(owned.T, ortho_factor)
    right_factor = lax.psum(trans_part, ("replica", "fsdp")) / replicas
    full_basis = normalize_full(right_factor)
    own_width = basis.shape[1]
    new_basis = lax.dynamic_slice_in_dim(
        full_basis, lax.axis_index("fsdp") * own_width, own_width, 1
    )
    new_momentum = buffer - 0.05 * product(ortho_factor, right_factor.T)[None]
    scale_factor = 0.1 * math.sqrt(ROWS / COLS)
    new_weight = (
        weight.astype(jnp.float32) - scale_factor * product(ortho_factor, full_basis.T)
    ).astype(jnp.bfloat16)
    return (new_weight, new_momentum, new_basis)


def solution(mesh):
    return jax.shard_map(
        body,
        mesh=mesh,
        in_specs=(
            P("fsdp", "tensor"),
            P("replica", "fsdp", "tensor"),
            P("replica", "fsdp", "tensor"),
            P("tensor", "fsdp"),
        ),
        out_specs=(P("fsdp", "tensor"), P("replica", "fsdp", "tensor"), P("tensor", "fsdp")),
        check_vma=False,
    )
```

profile of v0, /device:TPU:1, one launch (start us, length us, event | category | flops | bytes accessed | tf_op | source)
XLA Modules:
  0.0 634.0 jit_solution(357509176000616062)
XLA Ops:
  7.2 0.0 all-gather.2.cloned.1.call-start
  7.2 0.7 all-gather.2.cloned.1.call-update
  7.9 0.0 all-reduce.5.cloned.1.call-start
  7.9 80.5 %all-gather.2.cloned.1.call-done = f32[2048,256]{0,1:T(8,128)} async-done(((f32[2048,8]{0,1:T(8,128)}), f32[2048,256]{0,1:T(8,128)}) %all-gather.2.cloned.1.call-update) | async-done | bytes 2097168 | tf_op jit(solution)/shard_map/all_gather | solution.py:31
  88.4 7.2 %fusion.2 = f32[448,256]{1,0:T(8,128)} fusion(f32[2048,256]{0,1:T(8,128)} %all-gather.2.cloned.1.call-done, f32[1,448,2048]{2,1,0:T(8,128)} %param.5, bf16[1,448,2048]{2,1,0:T(8,128)(2,1)} %param.6), kind=kOutput, calls=%fused_computation.5 | convolution fusion | flops 2820407296 | bytes 8060928 | tf_op jit(solution)/shard_map/dot_general | solution.py:13
  95.6 0.0 all-reduce.5.cloned.1.call-update
  95.6 0.0 all-reduce.7.cloned.1.call-start
  95.7 64.9 %all-reduce.5.cloned.1.call-done = f32[448,256]{1,0:T(8,128)} async-done(((f32[448,256]{1,0:T(8,128)}), f32[448,256]{1,0:T(8,128)}) %all-reduce.5.cloned.1.call-update) | async-done | bytes 458768 | tf_op jit(solution)/shard_map/psum | solution.py:32
  160.6 2.9 fusion.18
  163.5 0.0 all-reduce.7.cloned.1.call-update
  163.5 0.2 all-reduce.9.cloned.1.call-start
  163.7 1.1 broadcast_multiply_fusion
  164.8 141.1 %all-reduce.7.cloned.1.call-done = f32[256,256]{0,1:T(8,128)} async-done(((f32[256,256]{0,1:T(8,128)}), f32[256,256]{0,1:T(8,128)}) %all-reduce.7.cloned.1.call-update) | async-done | bytes 262160 | tf_op jit(solution)/shard_map/psum | solution.py:33
  305.9 1.1 copy.8
  307.0 1.0 fusion.6
  308.0 11.7 %cholesky.50 = f32[128,128]{1,0:T(8,128)S(1)} custom-call(f32[128,128]{1,0:T(8,128)S(1)} %cholesky.118), custom_call_target="Cholesky" | custom-call | tf_op jit(solution)/shard_map/jit(cholesky)/cholesky | solution.py:34
  319.7 9.8 %custom-call.14 = f32[1,128,128]{1,2,0:T(8,128)S(1)} custom-call(f32[1,128,128]{2,1,0:T(8,128)S(1)} %get-tuple-element.27), custom_call_target="InvertDiagBlocksLowerTriangular" | custom-call | tf_op jit(solution)/shard_map/jit(cholesky)/cholesky | solution.py:34
  329.6 0.2 constant_dynamic-update-slice_fusion
  329.8 0.3 convolution_subtract_fusion.1
  330.1 11.7 %cholesky.105 = f32[128,128]{1,0:T(8,128)S(1)} custom-call(f32[128,128]{1,0:T(8,128)S(1)} %convolution_subtract_fusion.1), custom_call_target="Cholesky" | custom-call | tf_op jit(solution)/shard_map/jit(cholesky)/cholesky | solution.py:34
  341.8 0.6 compare_reduce_fusion
  343.8 0.1 triangular_solve.58
  343.9 4.2 while.1
  344.0 0.6 fusion.27
  344.6 1.4 bitcast_dynamic-update-slice_fusion.2
  346.1 0.6 fusion.27
  346.6 1.4 bitcast_dynamic-update-slice_fusion.2
  348.0 19.7 %custom-call.15 = f32[2,128,128]{1,2,0:T(8,128)S(1)} custom-call(f32[2,128,128]{2,1,0:T(8,128)S(1)} %get-tuple-element.10), custom_call_target="InvertDiagBlocksLowerTriangular" | custom-call | tf_op jit(solution)/shard_map/triangular_solve | solution.py:17
  367.7 0.3 fusion.7
  368.1 0.4 convolution_subtract_fusion
  368.4 0.3 fusion.9
  368.8 0.0 copy-done.2
  368.8 0.0 copy-start.5
  368.8 10.2 %fusion = f32[2048,256]{1,0:T(8,128)} fusion(f32[1,448,2048]{2,1,0:T(8,128)} %param.5, bf16[1,448,2048]{2,1,0:T(8,128)(2,1)S(1)} %copy-done.2, f32[448,128]{1,0:T(8,128)S(1)} %fusion.9, f32[448,128]{1,0:T(8,128)S(1)} %fusion.7), kind=kOutput, calls=%fused_computation.3 | convolution fusion | flops 2820521984 | bytes 8060928 | tf_op jit(solution)/shard_map/dot_general | solution.py:13
  378.9 0.0 all-reduce.9.cloned.1.call-update
  379.0 224.2 %all-reduce.9.cloned.1.call-done = f32[2048,256]{1,0:T(8,128)} async-done(((f32[2048,256]{1,0:T(8,128)}), f32[2048,256]{1,0:T(8,128)}) %all-reduce.9.cloned.1.call-update) | async-done | bytes 2097168 | tf_op jit(solution)/shard_map/psum | solution.py:37
  603.2 2.0 multiply_reduce_fusion
  605.2 7.1 %psum.31 = f32[1,256]{1,0:T(1,128)S(1)} all-reduce(f32[1,256]{1,0:T(1,128)S(1)} %bitcast.43), channel_id=1, replica_groups=mesh['replica'=4,'fsdp'=32,'tensor'=2] {'tensor'}, use_global_device_ids=true, to_apply=%region_8.9 | all-reduce | flops 256 | bytes 2048 | tf_op jit(solution)/shard_map/psum | solution.py:23
  612.3 0.0 copy-done.1
  612.3 0.1 multiply_divide_fusion
  612.5 0.0 copy-start.4
  612.5 1.3 copy-done.4
  613.8 0.3 constant_dynamic-slice_fusion.1
  614.1 0.9 copy.9
  615.1 6.9 %subtract_convert_fusion = bf16[448,2048]{1,0:T(8,128)(2,1)} fusion(bf16[448,2048]{1,0:T(8,128)(2,1)} %param.4, f32[2048,256]{1,0:T(8,128)} %copy-done.4, f32[448,128]{1,0:T(8,128)} %copy-done.5, f32[448,128]{1,0:T(8,128)S(1)} %fusion.7), kind=kOutput, calls=%fused_computation.7 | convolution fusion | flops 2822356992 | bytes 6225920 | tf_op jit(solution)/shard_map/dot_general | solution.py:13
  621.9 0.0 copy-done
  621.9 0.0 copy-done.6
  621.9 5.5 bitcast_subtract_fusion
  (17 shorter events, 0.2 us)
Async XLA Ops:
  7.2 81.3 %all-gather.2.cloned.1.call-start = ((), (), s32[]{:S(2)}) async-start(), calls=%async_computation | async-start | bytes 2162688 | tf_op jit(solution)/shard_map/all_gather | solution.py:31
  7.9 152.7 %all-reduce.5.cloned.1.call-start = ((), (), s32[]{:S(2)}) async-start(), calls=%async_computation.1 | async-start | bytes 917504 | tf_op jit(solution)/shard_map/psum | solution.py:32
  95.6 210.3 %all-reduce.7.cloned.1.call-start = ((), (), s32[]{:S(2)}) async-start(), calls=%async_computation.2 | async-start | bytes 524288 | tf_op jit(solution)/shard_map/psum | solution.py:33
  163.5 439.7 %all-reduce.9.cloned.1.call-start = ((), (), s32[]{:S(2)}) async-start(), calls=%async_computation.3 | async-start | bytes 4194304 | tf_op jit(solution)/shard_map/psum | solution.py:37
  319.7 49.0 %copy-start.2 = (bf16[1,448,2048]{2,1,0:T(8,128)(2,1)S(1)}, bf16[1,448,2048]{2,1,0:T(8,128)(2,1)}, u32[]{:S(2)}) copy-start(bf16[1,448,2048]{2,1,0:T(8,128)(2,1)} %param.6) | copy-start | bytes 5505028
  368.8 10.2 %copy-start.5 = (f32[448,128]{1,0:T(8,128)}, f32[448,128]{1,0:T(8,128)S(1)}, u32[]{:S(2)}) copy-start(f32[448,128]{1,0:T(8,128)S(1)} %fusion.9) | copy-start | bytes 688132
  603.2 9.1 %copy-start.1 = (f32[2048,256]{1,0:T(8,128)S(1)}, f32[2048,256]{1,0:T(8,128)}, u32[]{:S(2)}) copy-start(f32[2048,256]{1,0:T(8,128)} %all-reduce.9.cloned.1.call-done) | copy-start | bytes 6291460
  612.5 1.3 copy-start.4
  615.1 6.9 %copy-start = (f32[1,448,2048]{2,1,0:T(8,128)S(1)}, f32[1,448,2048]{2,1,0:T(8,128)}, u32[]{:S(2)}) copy-start(f32[1,448,2048]{2,1,0:T(8,128)} %param.5) | copy-start | bytes 11010052
  615.1 6.9 %copy-start.3 = (bf16[1,448,2048]{2,1,0:T(8,128)(2,1)S(1)}, bf16[1,448,2048]{2,1,0:T(8,128)(2,1)}, u32[]{:S(2)}) copy-start(bf16[1,448,2048]{2,1,0:T(8,128)(2,1)} %param.6) | copy-start | bytes 5505028
  615.1 6.9 %copy-start.6 = (f32[448,128]{1,0:T(8,128)S(1)}, f32[448,128]{1,0:T(8,128)}, u32[]{:S(2)}) copy-start(f32[448,128]{1,0:T(8,128)} %copy-done.5) | copy-start | bytes 688132
Sparse Core Ops, SparseCore 0:
  10.6 77.7 all-gather.1
  95.7 64.7 all-reduce.4
  165.0 140.8 all-reduce.6
  379.1 224.0 all-reduce.8
where the time goes:
time: 634 us
  waiting for transfers between devices  511 us (81%)
  other arithmetic  57.9 us (9%)
  matrix products  34 us (5%)
  between operations  15.2 us (2%)
  local copies, waits for them, and re-layouts  7.73 us (1%)
  blocking collectives  7.08 us (1%)
    psum x1, waiting for transfers between devices, body(): right_factor = lax.psum(trans_part, ('replica', 'fsdp')) / replicas  224 us
    psum x1, waiting for transfers between devices, body(): gram_matrix = lax.psum(product(left_factor.T, left_factor), 'fsdp')  141 us
    all_gather x1, waiting for transfers between devices, body(): lax.all_gather(basis, 'fsdp', axis=1, tiled=True)  80.5 us
    psum x1, waiting for transfers between devices, body(): left_factor = lax.psum(partial_left, ('replica', 'tensor')) / replicas  64.9 us
    another operation x6, other arithmetic, body(): lower_factor = jnp.linalg.cholesky(gram_matrix)  33.9 us
    dot_general x5, matrix products, product(): return jnp.dot(first, second, precision=lax.Precision.HIGHEST)  32.6 us
    another operation x3, other arithmetic, solve_right(): lax.linalg.triangular_solve(lower_factor, values, left_side=False, lower=...  19.7 us
  transfers between devices with their start and end apart: 4, of which 4 were waited for; matrix products, arithmetic and copies ran while one was open for 0% of the time, Pallas kernels for 0%

commit v1 on v0

v1 whole, which is shorter than its diff:
```python
import math

import jax
import jax.numpy as jnp
from jax import lax
from jax.experimental import pallas as pl
from jax.experimental.pallas import tpu as pltpu
from jax.sharding import PartitionSpec as P

ROWS = 14336
COLS = 4096
RANK = 256
NX, NY, NZ = 4, 4, 8
MB = 448
NB = 2048
HALF = NB // 2
CH = 256
BLK = 64
MESH = pl.DeviceIdType.MESH
HIGH = lax.Precision.HIGHEST
F32 = jnp.float32

COUNT = {}
TOTAL = 0
for _name, _n in (
    ("ax", 3), ("az", 28), ("bz", 7), ("bx", 3),
    ("lc", 1), ("ly", 3), ("ly2", 3), ("lc2", 1),
    ("gx", 3), ("gz", 7), ("gx2", 3), ("gy2", 3), ("gc2", 1),
    ("wa1", 3), ("wb1", 12), ("wa2", 3), ("wb2", 3), ("w3", 7),
    ("wz", 7), ("wa5", 3), ("wb5", 3), ("wa6", 3), ("wb6", 3), ("n", 1),
):
    COUNT[_name] = TOTAL
    TOTAL += _n


def dot(a, b, dims):
    return lax.dot_general(a, b, (dims, ((), ())), precision=HIGH, preferred_element_type=F32)


def nn(a, b):
    return dot(a, b, ((1,), (0,)))


def nt(a, b):
    return dot(a, b, ((1,), (1,)))


def tn(a, b):
    return dot(a, b, ((0,), (0,)))


def pivots(done, t):
    top, rest = t[0:8], t[8:]
    below = lax.broadcasted_iota(jnp.int32, (8, 1), 0)
    left = lax.broadcasted_iota(jnp.int32, (BLK - 8, 1), 0) < BLK - 8 - 8 * done
    for k in range(8):
        rs = lax.rsqrt(top[k : k + 1, k : k + 1])
        row = top[k : k + 1, :] * rs
        col = jnp.where(below > k, top[:, k : k + 1] * rs, 0.0)
        low = jnp.where(left, rest[:, k : k + 1] * rs, 0.0)
        top = jnp.where(below == k, row, top - col * row)
        rest = rest - low * row
    return pltpu.roll(jnp.concatenate([rest, top], axis=0), 2 * BLK - 8, 1)


def chol_block(b, a_ref, li_ref):
    r0 = BLK * b
    w0 = 2 * BLK * (b // 2)
    odd = b % 2
    lane = lax.broadcasted_iota(jnp.int32, (BLK, 2 * BLK), 1)
    row = lax.broadcasted_iota(jnp.int32, (BLK, 2 * BLK), 0)
    t = a_ref[r0 : r0 + BLK, w0 : w0 + 2 * BLK]
    if odd:
        t = pltpu.roll(t, BLK, 1)
    t = jnp.where(lane < BLK, t, jnp.where(lane - BLK == row, 1.0, 0.0))
    t = lax.fori_loop(0, BLK // 8, pivots, t)
    inv = jnp.where(lane < BLK, t, 0.0)
    if odd:
        inv = pltpu.roll(inv, BLK, 1)
    u = nn(inv, a_ref[w0 : w0 + 2 * BLK, :])
    ul = nn(inv, li_ref[w0 : w0 + 2 * BLK, :])
    if r0 + BLK < RANK:
        rows = lax.broadcasted_iota(jnp.int32, (RANK, 1), 0)
        a_ref[...] = a_ref[...] - tn(u, u)
        li_ref[...] = jnp.where(rows >= r0 + BLK, li_ref[...] - tn(u, ul), li_ref[...])
    li_ref[r0 : r0 + BLK, :] = ul


def kernel(
    mom_hbm, grad_hbm, bas_in,
    right_out, ortho_out, norm_out, newb_out,
    buf, gra, bas, lpart, lrc, lry, left, leftT, gpart, grx, grz, gram, linv,
    w, ra1, rb1, sa1, sb1, ra2, rb2, s2, r3, wf, nown, nrec,
    lsem, ssem, rsem,
):
    y = lax.axis_index("replica")
    f = lax.axis_index("fsdp")
    core = lax.axis_index("tensor")
    x, z = f // NZ, f % NZ

    def xp(d):
        return (y, lax.rem(x + d + NX, NX) * NZ + z, core)

    def yp(d):
        return (lax.rem(y + d + NY, NY), f, core)

    def zp(d):
        return (y, x * NZ + lax.rem(z + d + NZ, NZ), core)

    cp = (y, f, 1 - core)

    load_m = pltpu.make_async_copy(mom_hbm, buf, lsem.at[0])
    load_g = pltpu.make_async_copy(grad_hbm, gra, lsem.at[1])
    load_m.start()
    load_g.start()

    sent = []

    def make(src, dst, name, n, dev):
        k = COUNT[name] + n
        return pltpu.make_async_remote_copy(
            src_ref=src, dst_ref=dst, send_sem=ssem.at[k], recv_sem=rsem.at[k],
            device_id=dev, device_id_type=MESH,
        )

    def send(*args):
        copy = make(*args)
        copy.start()
        sent.append(copy)
        return copy

    bas[0, x, z] = bas_in[:, :HALF]
    bas[1, x, z] = bas_in[:, HALF:]

    barrier = pltpu.get_barrier_semaphore()
    peers = [xp(d) for d in range(1, NX)] + [yp(d) for d in range(1, NY)]
    peers += [zp(d) for d in range(1, NZ)] + [cp]
    for dev in peers:
        pl.semaphore_signal(barrier, inc=1, device_id=dev, device_id_type=MESH)
    pl.semaphore_wait(barrier, len(peers))

    def ring(way, step, i):
        piece = bas.at[0, lax.rem(x - i + NX, NX), lax.rem(z - way * (step - 1) + NZ, NZ)]
        return send(piece, piece, "az", (16 if way < 0 else 0) + (step - 1) * 4 + i, zp(way))

    hops = {}
    mine = bas.at[0, x, z]
    ax = [send(mine, mine, "ax", d - 1, xp(d)) for d in range(1, NX)]
    hops[1, 1, 0] = ring(1, 1, 0)
    hops[-1, 1, 0] = ring(-1, 1, 0)
    mine = bas.at[1, x, z]
    bz = [send(mine, mine, "bz", d - 1, zp(d)) for d in range(1, NZ)]
    for i in range(1, NX):
        ax[i - 1].wait_recv()
        hops[1, 1, i] = ring(1, 1, i)
        hops[-1, 1, i] = ring(-1, 1, i)
    for copy in bz:
        copy.wait_recv()
    mine = bas.at[1, x]
    bx = [send(mine, mine, "bx", d - 1, xp(d)) for d in range(1, NX)]
    for step in range(2, 5):
        for i in range(NX):
            for way in (1, -1):
                if (way, step - 1, i) in hops:
                    hops.pop((way, step - 1, i)).wait_recv()
                if way == 1 or step < 4:
                    hops[way, step, i] = ring(way, step, i)
    load_m.wait()
    load_g.wait()
    for r in range(0, MB, 64):
        rows = slice(r, r + 64)
        buf[rows, :] = buf[rows, :] + gra[rows, :].astype(F32)
    for copy in list(hops.values()) + bx:
        copy.wait_recv()

    lpart[...] = jnp.zeros_like(lpart)
    for h in range(2):

        @pl.loop(0, HALF // CH)
        def _(c):
            at = pl.multiple_of(c * CH, CH)
            part = bas[h, :, :, :, pl.ds(at, CH)].reshape(RANK, CH)
            lpart[...] += nt(buf[:, pl.ds(pl.multiple_of(h * HALF + at, CH), CH)], part)

    hm, qm = MB // 2, MB // 8
    own = pl.multiple_of(core * hm, 8)
    other = pl.multiple_of((1 - core) * hm, 8)
    lc = send(lpart.at[pl.ds(other, hm)], lrc, "lc", 0, cp)
    lc.wait_recv()
    lpart[pl.ds(own, hm), :] = lpart[pl.ds(own, hm), :] + lrc[...]

    def quarter(q):
        return pl.ds(pl.multiple_of(own + q * qm, 8), qm)

    ly = [
        send(lpart.at[quarter(lax.rem(y + d, NY))], lry.at[d - 1], "ly", d - 1, yp(d))
        for d in range(1, NY)
    ]
    for copy in ly:
        copy.wait_recv()
    left[quarter(y), :] = (lpart[quarter(y), :] + lry[0] + lry[1] + lry[2]) * 0.25
    mine = left.at[quarter(y)]
    ly2 = [send(mine, mine, "ly2", d - 1, yp(d)) for d in range(1, NY)]
    for copy in ly2:
        copy.wait_recv()
    mine = left.at[pl.ds(own, hm)]
    lc2 = send(mine, mine, "lc2", 0, cp)
    lc2.wait_recv()

    leftT[...] = left[...].T
    gpart[...] = nt(leftT[...], leftT[...])
    g0 = core * 128 + y * 32

    def grows(base, n):
        return pl.ds(pl.multiple_of(base, 8), n)

    gx = [
        send(gpart.at[grows(g0 + 8 * lax.rem(x + d, NX), 8)], grx.at[d - 1], "gx", d - 1, xp(d))
        for d in range(1, NX)
    ]

    wa1, wb1 = [], []

    def product(h, g):
        at = pl.multiple_of(h * HALF + g * CH, CH)
        w[h, g] = nn(leftT[...], buf[:, pl.ds(at, CH)])

    def yrows(q):
        return pl.ds(pl.multiple_of(q * 64, 64), 64)

    for i in (1, 2, 3, 0):
        g = lax.rem(x + i, NX)
        product(0, g)
        if i:
            wa1.append(send(w.at[0, g], ra1.at[i - 1], "wa1", i - 1, xp(i)))
        product(1, i)
        for d in range(1, NY):
            wb1.append(
                send(w.at[1, i, yrows(lax.rem(y + d, NY))], rb1.at[d - 1, i], "wb1",
                     (d - 1) * 4 + i, yp(d))
            )

    for copy in gx:
        copy.wait_recv()
    mine = grows(g0 + 8 * x, 8)
    grz[z] = gpart[mine, :] + grx[0] + grx[1] + grx[2]
    gz = [send(grz.at[z], grz.at[z], "gz", d - 1, zp(d)) for d in range(1, NZ)]
    for copy in gz:
        copy.wait_recv()
    total = grz[0]
    for k in range(1, NZ):
        total = total + grz[k]
    gram[mine, :] = total
    part = gram.at[mine]
    gx2 = [send(part, part, "gx2", d - 1, xp(d)) for d in range(1, NX)]
    for copy in gx2:
        copy.wait_recv()
    part = gram.at[grows(g0, 32)]
    gy2 = [send(part, part, "gy2", d - 1, yp(d)) for d in range(1, NY)]
    for copy in gy2:
        copy.wait_recv()
    part = gram.at[grows(core * 128, 128)]
    gc2 = send(part, part, "gc2", 0, cp)
    gc2.wait_recv()

    for copy in wa1:
        copy.wait_recv()
    sa1[...] = w[0, x] + ra1[0] + ra1[1] + ra1[2]
    wa2 = [
        send(sa1.at[yrows(lax.rem(y + d, NY))], ra2.at[d - 1], "wa2", d - 1, yp(d))
        for d in range(1, NY)
    ]
    for copy in wb1:
        copy.wait_recv()
    for g in range(NX):
        sb1[g] = w[1, g, yrows(y), :] + rb1[0, g] + rb1[1, g] + rb1[2, g]
    wb2 = [
        send(sb1.at[lax.rem(x + d, NX)], rb2.at[d - 1], "wb2", d - 1, xp(d)) for d in range(1, NX)
    ]

    for copy in gx2 + gy2 + [gc2]:
        copy.wait_send()
    sent[:] = [copy for copy in sent if not any(copy is c for c in gx2 + gy2 + [gc2])]
    rows = lax.broadcasted_iota(jnp.int32, (RANK, RANK), 0)
    cols = lax.broadcasted_iota(jnp.int32, (RANK, RANK), 1)
    linv[...] = jnp.where(rows == cols, 1.0, 0.0)
    chol_block(0, gram, linv)

    for copy in wa2 + wb2:
        copy.wait_recv()
    s2[0] = sa1[yrows(y), :] + ra2[0] + ra2[1] + ra2[2]
    s2[1] = sb1[x] + rb2[0] + rb2[1] + rb2[2]

    def zrows(q):
        return pl.ds(pl.multiple_of(q * 8, 8), 8)

    w3 = [
        send(s2.at[:, zrows(lax.rem(z + d, NZ))], r3.at[d - 1], "w3", d - 1, zp(d))
        for d in range(1, NZ)
    ]
    chol_block(1, gram, linv)

    for copy in w3:
        copy.wait_recv()
    total = s2[:, zrows(z), :]
    for k in range(NZ - 1):
        total = total + r3[k]
    mine = pl.ds(pl.multiple_of(y * 64 + z * 8, 8), 8)
    wf[:, x, mine, :] = total
    part = wf.at[:, x, mine]
    wz = [send(part, part, "wz", d - 1, zp(d)) for d in range(1, NZ)]
    for copy in wz:
        copy.wait_recv()
    part = wf.at[0, x, yrows(y)]
    wa5 = [send(part, part, "wa5", d - 1, yp(d)) for d in range(1, NY)]
    part = wf.at[1, x, yrows(y)]
    wb5 = [send(part, part, "wb5", d - 1, xp(d)) for d in range(1, NX)]
    chol_block(2, gram, linv)
    for copy in wa5 + wb5:
        copy.wait_recv()
    part = wf.at[0, x]
    wa6 = [send(part, part, "wa6", d - 1, xp(d)) for d in range(1, NX)]
    part = wf.at[1, :, yrows(y)]
    wb6 = [send(part, part, "wb6", d - 1, yp(d)) for d in range(1, NY)]
    chol_block(3, gram, linv)
    ortho_out[...] = nt(left[...], linv[...])
    for copy in wa6 + wb6:
        copy.wait_recv()

    nown[...] = jnp.zeros_like(nown)
    for h in range(2):

        @pl.loop(0, NX)
        def _(g):
            part = nn(linv[...], wf[h, g] * 0.25)
            right_out[:, pl.ds(pl.multiple_of(h * HALF + g * CH, CH), CH)] = part
            sq = part * part
            nown[...] += sq[:, :128] + sq[:, 128:]

    ns = send(nown, nrec, "n", 0, cp)
    ns.wait_recv()
    norms = jnp.sqrt(jnp.sum(nown[...] + nrec[...], axis=1, keepdims=True) + 1e-06)
    norm_out[...] = jnp.broadcast_to(norms, (RANK, 128))
    mine = pl.ds(pl.multiple_of(f * 8, 8), 8)
    newb_out[...] = right_out[mine, :] / norm_out[mine, 0:1]

    for copy in sent:
        copy.wait_send()


def factors(momentum, grad, basis_t):
    v = pltpu.VMEM
    any_ = pl.BlockSpec(memory_space=pl.ANY)
    vm = pl.BlockSpec(memory_space=pltpu.VMEM)
    return pl.pallas_call(
        kernel,
        out_shape=(
            jax.ShapeDtypeStruct((RANK, NB), F32),
            jax.ShapeDtypeStruct((MB, RANK), F32),
            jax.ShapeDtypeStruct((RANK, 128), F32),
            jax.ShapeDtypeStruct((8, NB), F32),
        ),
        in_specs=[any_, any_, vm],
        out_specs=(vm, vm, vm, vm),
        scratch_shapes=[
            v((MB, NB), F32), v((MB, NB), jnp.bfloat16), v((2, NX, NZ, 8, HALF), F32),
            v((MB, RANK), F32), v((MB // 2, RANK), F32), v((3, MB // 8, RANK), F32),
            v((MB, RANK), F32), v((RANK, MB), F32),
            v((RANK, RANK), F32), v((3, 8, RANK), F32), v((NZ, 8, RANK), F32),
            v((RANK, RANK), F32), v((RANK, RANK), F32),
            v((2, NX, RANK, CH), F32), v((3, RANK, CH), F32), v((3, NX, 64, CH), F32),
            v((RANK, CH), F32), v((NX, 64, CH), F32),
            v((3, 64, CH), F32), v((3, 64, CH), F32), v((2, 64, CH), F32),
            v((7, 2, 8, CH), F32), v((2, NX, RANK, CH), F32),
            v((RANK, 128), F32), v((RANK, 128), F32),
            pltpu.SemaphoreType.DMA((2,)),
            pltpu.SemaphoreType.DMA((TOTAL,)),
            pltpu.SemaphoreType.DMA((TOTAL,)),
        ],
        compiler_params=pltpu.CompilerParams(
            collective_id=0, has_side_effects=True, vmem_limit_bytes=48 * 1024 * 1024
        ),
        name="factors",
    )(momentum, grad, basis_t)


def update_kernel(ortho, right, norm, mom, grad, weight, new_mom, new_w):
    scale = 0.1 * math.sqrt(ROWS / COLS)
    part = right[...]
    buffer = mom[...] + grad[...].astype(F32)
    new_mom[...] = buffer - 0.05 * nn(ortho[...], part)
    delta = nn(ortho[...], part / norm[:, 0:1])
    new_w[...] = (weight[...].astype(F32) - scale * delta).astype(jnp.bfloat16)


def update(ortho, right, norm, momentum, grad, weight):
    cols = pl.BlockSpec((MB, CH), lambda i: (0, i))
    return pl.pallas_call(
        update_kernel,
        grid=(NB // CH,),
        out_shape=(
            jax.ShapeDtypeStruct((MB, NB), F32),
            jax.ShapeDtypeStruct((MB, NB), jnp.bfloat16),
        ),
        in_specs=[
            pl.BlockSpec((MB, RANK), lambda i: (0, 0)),
            pl.BlockSpec((RANK, CH), lambda i: (0, i)),
            pl.BlockSpec((RANK, 128), lambda i: (0, 0)),
            cols, cols, cols,
        ],
        out_specs=(cols, cols),
        compiler_params=pltpu.CompilerParams(vmem_limit_bytes=32 * 1024 * 1024),
        name="update",
    )(ortho, right, norm, momentum, grad, weight)


def body(weight, momentum, grad, basis):
    right, ortho, norm, new_basis_t = factors(momentum[0], grad[0], basis.T)
    new_momentum, new_weight = update(ortho, right, norm, momentum[0], grad[0], weight)
    return new_weight, new_momentum[None], new_basis_t.T


def solution(mesh):
    return jax.shard_map(
        body,
        mesh=mesh,
        in_specs=(
            P("fsdp", "tensor"),
            P("replica", "fsdp", "tensor"),
            P("replica", "fsdp", "tensor"),
            P("tensor", "fsdp"),
        ),
        out_specs=(P("fsdp", "tensor"), P("replica", "fsdp", "tensor"), P("tensor", "fsdp")),
        check_vma=False,
    )
```

time: 634 us -> 134 us (0.21)
  waiting for transfers between devices: 511 us -> 0 us
  Pallas kernels: 0 us -> 130 us
  other arithmetic: 57.9 us -> 0 us
  matrix products: 34 us -> 0 us
  between operations: 15.2 us -> 0.67 us
  blocking collectives: 7.08 us -> 0 us
    psum x3 -> x0, waiting for transfers between devices: 430 us -> none  [the longest x1 224 us: body(): right_factor = lax.psum(trans_part, ('replica', 'fsdp')) / replicas]
    pallas_call x0 -> x2, Pallas kernels: none -> 130 us  [the longest x1 120 us: factors(): pl.pallas_call(kernel, out_shape=(jax.ShapeDtypeStruct((RANK, NB), F32),...]
    all_gather x1 -> x0, waiting for transfers between devices: 80.5 us -> none  [body(): lax.all_gather(basis, 'fsdp', axis=1, tiled=True)]
    another operation x9 -> x0, other arithmetic: 53.7 us -> none  [the longest x6 33.9 us: body(): lower_factor = jnp.linalg.cholesky(gram_matrix)]
    dot_general x5 -> x0, matrix products: 32.6 us -> none  [product(): return jnp.dot(first, second, precision=lax.Precision.HIGHEST)]
    psum x1 -> x0, blocking collectives: 7.08 us -> none  [normalize_full(): lax.psum(jnp.sum(right_factor * right_factor, axis=0, keepdims=True), 'te...]
  transfers between devices with their start and end apart: 4 -> 0, of which waited for: 4 -> 0; matrix products, arithmetic and copies ran while one was open for 0% -> 0% of each run, Pallas kernels for 0% -> 0%
where the time goes in v1:
time: 134 us
  Pallas kernels  130 us (97%)
  local copies, waits for them, and re-layouts  2.97 us (2%)
    pallas_call x1, Pallas kernels, factors(): pl.pallas_call(kernel, out_shape=(jax.ShapeDtypeStruct((RANK, NB), F32),...  120 us
    pallas_call x1, Pallas kernels, update(): pl.pallas_call(update_kernel, grid=(NB // CH,), out_shape=(jax.ShapeDtype...  10 us
    unnamed x9, local copies, waits for them, and re-layouts  2.97 us

profile of v1, /device:TPU:1, one launch (start us, length us, event | category | flops | bytes accessed | tf_op | source)
XLA Modules:
  0.0 133.5 jit_solution(118556930460751516)
XLA Ops:
  0.6 0.0 copy-start.1
  0.6 1.5 %copy-done.1 = bf16[1,448,2048]{2,1,0:T(8,128)(2,1)S(1)} copy-done((bf16[1,448,2048]{2,1,0:T(8,128)(2,1)S(1)}, bf16[1,448,2048]{2,1,0:T(8,128)(2,1)}, u32[]{:S(2)}) %copy-start.1) | copy-done | bytes 1835032
  2.1 0.0 copy-start.3
  2.1 0.8 copy-done.3
  3.0 0.0 copy-start
  3.0 0.0 copy-start.2
  3.0 119.9 %factors.1 = (f32[256,2048]{1,0:T(8,128)S(1)}, f32[448,256]{1,0:T(8,128)S(1)}, f32[256,128]{1,0:T(8,128)S(1)}, f32[8,2048]{1,0:T(8,128)S(1)}) custom-call(f32[448,2048]{1,0:T(8,128)} %bitcast.5, bf16[448,2048]{1,0:T(8,128)(2,1)S(1)} %bitcast.7, f32[8,2048]{1,0:T(8,128)S(1)} %bitcast.9), custom_call_target="tpu_custom_call" | custom-call | tf_op jit(solution)/shard_map/factors/pallas_call | solution.py:355
  122.8 0.0 copy-done
  122.9 0.0 copy-done.2
  122.9 10.0 %update.1 = (f32[448,2048]{1,0:T(8,128)}, bf16[448,2048]{1,0:T(8,128)(2,1)}) custom-call(f32[448,256]{1,0:T(8,128)S(1)} %get-tuple-element.9.ortho, f32[256,2048]{1,0:T(8,128)S(1)} %get-tuple-element.10.right, f32[256,128]{1,0:T(8,128)S(1)} %get-tuple-element.11.norm, f32[448,2048]{1,0:T(8,128)S(1)} %bitcast.6, bf16[448,2048]{1,0:T(8,128)(2,1)S(1)} %bitcast.8, ...), custom_call_target="tpu_custom_call" | custom-call | tf_op jit(solution)/shard_map/update/pallas_call | solution.py:398
  132.9 0.6 copy.8
Async XLA Ops:
  0.6 1.5 %copy-start.1 = (bf16[1,448,2048]{2,1,0:T(8,128)(2,1)S(1)}, bf16[1,448,2048]{2,1,0:T(8,128)(2,1)}, u32[]{:S(2)}) copy-start(bf16[1,448,2048]{2,1,0:T(8,128)(2,1)} %param.6) | copy-start | bytes 5505028
  2.1 0.8 copy-start.3
  3.0 119.9 %copy-start = (f32[1,448,2048]{2,1,0:T(8,128)S(1)}, f32[1,448,2048]{2,1,0:T(8,128)}, u32[]{:S(2)}) copy-start(f32[1,448,2048]{2,1,0:T(8,128)} %param.5) | copy-start | bytes 11010052
  3.0 119.9 %copy-start.2 = (bf16[448,2048]{1,0:T(8,128)(2,1)S(1)}, bf16[448,2048]{1,0:T(8,128)(2,1)}, u32[]{:S(2)}) copy-start(bf16[448,2048]{1,0:T(8,128)(2,1)} %weight.1) | copy-start | bytes 5505028

commit v2 on v1

v2 whole, which is shorter than its diff:
```python
import math

import jax
import jax.numpy as jnp
from jax import lax
from jax.experimental import pallas as pl
from jax.experimental.pallas import tpu as pltpu
from jax.sharding import PartitionSpec as P

ROWS = 14336
COLS = 4096
RANK = 256
NX, NY, NZ = 4, 4, 8
MB = 448
NB = 2048
HALF = NB // 2
CH = 256
LN = CH // 2
BLK = 64
MESH = pl.DeviceIdType.MESH
HIGH = lax.Precision.HIGHEST
F32 = jnp.float32
BF16 = jnp.bfloat16
SCHEDULE = (1, 2, 2, 2, 2, 2)

COUNT, COUNTS = {}, {}
TOTAL = 0
for _name, _n in (
    ("ax", 3), ("az", 28), ("bz", 7), ("bx", 3),
    ("lc", 1), ("ly", 3), ("ly2", 3), ("lc2", 1),
    ("gp", 32), ("gz", 7), ("gp2", 32),
    ("wa1", 12), ("wb1", 12), ("wa2", 6), ("wb2", 6), ("w3", 14),
    ("wz", 14), ("wa5", 6), ("wb5", 6), ("wa6", 12), ("wb6", 12), ("n", 1),
):
    COUNT[_name], COUNTS[_name] = TOTAL, _n
    TOTAL += _n


def dot(a, b, dims):
    return lax.dot_general(a, b, (dims, ((), ())), precision=HIGH, preferred_element_type=F32)


def split(v):
    hi = v.astype(BF16)
    return hi, (v - hi.astype(F32)).astype(BF16)


def dot3(a, b, dims):
    def one(p, q):
        return lax.dot_general(p, q, (dims, ((), ())), preferred_element_type=F32)

    return one(a[0], b[0]) + (one(a[0], b[1]) + one(a[1], b[0]))


NN, NT = ((1,), (0,)), ((1,), (1,))


def nn(a, b):
    return dot(a, b, ((1,), (0,)))


def nt(a, b):
    return dot(a, b, ((1,), (1,)))


def tn(a, b):
    return dot(a, b, ((0,), (0,)))


def pivots(done, t):
    shape = (8, 2 * BLK)
    top, rest = t[0:8], t[8:]
    row = lax.broadcasted_iota(jnp.int32, shape, 0)
    lane = lax.broadcasted_iota(jnp.int32, shape, 1)
    cols = [jnp.broadcast_to(top[:, k : k + 1], shape) for k in range(8)]
    for k in range(8):
        rs = lax.rsqrt(jnp.broadcast_to(cols[k][k : k + 1, :], shape))
        col = jnp.where(row > k, cols[k] * rs, 0.0)
        own = jnp.broadcast_to(top[k : k + 1, :], shape) * rs
        top = jnp.where(row == k, own, top - col * own)
        for m in range(k + 1, 8):
            cols[m] = cols[m] - col * (jnp.broadcast_to(cols[m][k : k + 1, :], shape) * rs)
    low = jnp.where(lane < BLK - 8 * done, top, 0.0).T
    for k in range(8):
        rest = rest - low[8:BLK, k : k + 1] * top[k : k + 1, :]
    return pltpu.roll(jnp.concatenate([rest, top], axis=0), 2 * BLK - 8, 1)


def cholesky(a_ref, li_ref):
    lane = lax.broadcasted_iota(jnp.int32, (BLK, 2 * BLK), 1)
    row = lax.broadcasted_iota(jnp.int32, (BLK, 2 * BLK), 0)
    for b in range(RANK // BLK):
        r0 = BLK * b
        w0 = 2 * BLK * (b // 2)
        odd = b % 2
        t = a_ref[r0 : r0 + BLK, w0 : w0 + 2 * BLK]
        if odd:
            t = pltpu.roll(t, BLK, 1)
        t = jnp.where(lane < BLK, t, jnp.where(lane - BLK == row, 1.0, 0.0))
        t = lax.fori_loop(0, BLK // 16, pivots, t)
        yield
        t = lax.fori_loop(BLK // 16, BLK // 8, pivots, t)
        yield
        inv = jnp.where(lane < BLK, t, 0.0)
        if odd:
            inv = pltpu.roll(inv, BLK, 1)
        wide = slice(0, 2 * BLK) if b < 2 else slice(0, RANK)
        ul = nn(inv, li_ref[w0 : w0 + 2 * BLK, wide])
        if r0 + BLK < RANK:
            low = slice(0, RANK) if b == 0 else slice(RANK // 2, RANK)
            u = nn(inv, a_ref[w0 : w0 + 2 * BLK, low])
            rows = lax.broadcasted_iota(jnp.int32, (low.stop - low.start, 1), 0) + low.start
            a_ref[low, low] = a_ref[low, low] - tn(u, u)
            old = li_ref[low, wide]
            li_ref[low, wide] = jnp.where(rows >= r0 + BLK, old - tn(u, ul), old)
        li_ref[r0 : r0 + BLK, wide] = ul
        yield


def kernel(
    mom_hbm, grad_hbm, bas_in,
    right_out, ortho_out, norm_out, newb_out,
    buf, gra, bhi, blo, bas, lpart, lrc, lry, left, thi, tlo, gpart, grx, grz, gram, linv,
    w, rla, rlb, ra1, rb1, sa1, sb1, ra2, rb2, s2, r3, wf, nown, nrec,
    lsem, ssem, rsem,
):
    y = lax.axis_index("replica")
    f = lax.axis_index("fsdp")
    core = lax.axis_index("tensor")
    x, z = f // NZ, f % NZ

    def xp(d):
        return (y, lax.rem(x + d + NX, NX) * NZ + z, core)

    def yp(d):
        return (lax.rem(y + d + NY, NY), f, core)

    def zp(d):
        return (y, x * NZ + lax.rem(z + d + NZ, NZ), core)

    cp = (y, f, 1 - core)

    load_m = pltpu.make_async_copy(mom_hbm, buf, lsem.at[0])
    load_g = pltpu.make_async_copy(grad_hbm, gra, lsem.at[1])
    load_m.start()
    load_g.start()

    sent = []

    def make(src, dst, name, n, dev):
        k = COUNT[name] + n
        return pltpu.make_async_remote_copy(
            src_ref=src, dst_ref=dst, send_sem=ssem.at[k], recv_sem=rsem.at[k],
            device_id=dev, device_id_type=MESH,
        )

    def send(*args):
        copy = make(*args)
        copy.start()
        sent.append(copy)
        return copy

    bas[0, x, z] = bas_in[:, :HALF]
    bas[1, x, z] = bas_in[:, HALF:]

    barrier = pltpu.get_barrier_semaphore()
    plane = {}
    for n in range(1, 2 * NX * NY):
        dx, dy, dc = n // 8, n // 2 % NY, n % 2
        plane[n] = (
            lax.rem(x + dx, NX), lax.rem(y + dy, NY), lax.rem(core + dc, 2),
        )

    def pp(n):
        px, py, pc = plane[n]
        return (py, px * NZ + z, pc)

    peers = [zp(d) for d in range(1, NZ)] + [pp(n) for n in plane]
    for dev in peers:
        pl.semaphore_signal(barrier, inc=1, device_id=dev, device_id_type=MESH)
    load_m.wait()
    load_g.wait()

    @pl.loop(0, MB // 16)
    def _(r):
        rows = pl.ds(pl.multiple_of(r * 16, 16), 16)
        hi, lo = split(buf[rows, :] + gra[rows, :].astype(F32))
        bhi[rows, :] = hi
        blo[rows, :] = lo

    pl.semaphore_wait(barrier, len(peers))

    def ring(way, step, i):
        piece = bas.at[0, lax.rem(x - i + NX, NX), lax.rem(z - way * (step - 1) + NZ, NZ)]
        return send(piece, piece, "az", (16 if way < 0 else 0) + (step - 1) * 4 + i, zp(way))

    hops = {}
    mine = bas.at[0, x, z]
    ax = [send(mine, mine, "ax", d - 1, xp(d)) for d in range(1, NX)]
    hops[1, 1, 0] = ring(1, 1, 0)
    hops[-1, 1, 0] = ring(-1, 1, 0)
    mine = bas.at[1, x, z]
    bz = [send(mine, mine, "bz", d - 1, zp(d)) for d in range(1, NZ)]
    for i in range(1, NX):
        ax[i - 1].wait_recv()
        hops[1, 1, i] = ring(1, 1, i)
        hops[-1, 1, i] = ring(-1, 1, i)
    for copy in bz:
        copy.wait_recv()
    mine = bas.at[1, x]
    bx = [send(mine, mine, "bx", d - 1, xp(d)) for d in range(1, NX)]
    for step in range(2, 5):
        for i in range(NX):
            for way in (1, -1):
                if (way, step - 1, i) in hops:
                    hops.pop((way, step - 1, i)).wait_recv()
                if way == 1 or step < 4:
                    hops[way, step, i] = ring(way, step, i)
    for copy in list(hops.values()) + bx:
        copy.wait_recv()

    hm, qm = MB // 2, MB // 8
    own = pl.multiple_of(core * hm, 16)
    other = pl.multiple_of((1 - core) * hm, 16)

    def left_rows(at):
        rows = pl.ds(at, hm)
        for h in range(2):
            for c in range(0, HALF, 512):
                cols = slice(h * HALF + c, h * HALF + c + 512)
                part = split(bas[h, :, :, :, c : c + 512].reshape(RANK, 512))
                part = dot3((bhi[rows, cols], blo[rows, cols]), part, NT)
                lpart[rows, :] = part if h + c == 0 else lpart[rows, :] + part

    left_rows(other)
    lc = send(lpart.at[pl.ds(other, hm)], lrc, "lc", 0, cp)
    left_rows(own)
    lc.wait_recv()
    lpart[pl.ds(own, hm), :] = lpart[pl.ds(own, hm), :] + lrc[...]

    def quarter(q):
        return pl.ds(pl.multiple_of(own + q * qm, 8), qm)

    ly = [
        send(lpart.at[quarter(lax.rem(y + d, NY))], lry.at[d - 1], "ly", d - 1, yp(d))
        for d in range(1, NY)
    ]
    for copy in ly:
        copy.wait_recv()
    left[quarter(y), :] = (lpart[quarter(y), :] + lry[0] + lry[1] + lry[2]) * 0.25
    mine = left.at[quarter(y)]
    ly2 = [send(mine, mine, "ly2", d - 1, yp(d)) for d in range(1, NY)]

    def grows(base, n):
        return pl.ds(pl.multiple_of(base, 8), n)

    gpart[...] = tn(left[quarter(y), :], left[quarter(y), :])
    gp = []
    for n, (px, py, pc) in plane.items():
        part = gpart.at[grows(128 * pc + 32 * py + 8 * px, 8)]
        gp.append(send(part, grx.at[n], "gp", n, pp(n)))

    for copy in ly2:
        copy.wait_recv()
    mine = left.at[pl.ds(own, hm)]
    lc2 = send(mine, mine, "lc2", 0, cp)

    def yrows(q):
        return pl.ds(pl.multiple_of(q * 64, 64), 64)

    def zrows(q):
        return pl.ds(pl.multiple_of(q * 8, 8), 8)

    def turned(at):
        hi, lo = split(left[pl.ds(at, hm), :].T)
        thi[...] = hi
        tlo[...] = lo

    def half_product(at, h, g):
        cols = pl.ds(pl.multiple_of(h * HALF + g * CH, CH), CH)
        rows = pl.ds(at, hm)
        return dot3((thi[...], tlo[...]), (bhi[rows, cols], blo[rows, cols]), NN)

    turned(own)
    for h in range(2):
        for g in range(NX):
            part = half_product(own, h, g)
            w[h, g, 0] = part[:, :LN]
            w[h, g, 1] = part[:, LN:]
    lc2.wait_recv()
    turned(other)

    def product(h, g):
        part = half_product(other, h, g)
        w[h, g, 0] = w[h, g, 0] + part[:, :LN]
        w[h, g, 1] = w[h, g, 1] + part[:, LN:]

    xr, xl, xo = lax.rem(x + 1, NX), lax.rem(x + 3, NX), lax.rem(x + 2, NX)
    yr, yl, yo = (yrows(lax.rem(y + d, NY)) for d in (1, 3, 2))
    me = yrows(y)
    top, low = slice(0, RANK // 2), slice(RANK // 2, RANK)
    one, two = slice(0, NX // 2), slice(NX // 2, NX)
    A, B = {}, {}

    def to(name, store, c, n, src, dst, dev):
        store[name, c, n] = send(src, dst, name, c * (COUNTS[name] // 2) + n, dev)

    def taken(name, store, c, ns):
        for n in ns:
            store[name, c, n].wait_recv()

    product(0, xo)
    for c in range(2):
        to("wa1", A, c, 0, w.at[0, xo, c, top], rla.at[c, 0], xp(1))
        to("wa1", A, c, 1, w.at[0, xo, c, low], rla.at[c, 1], xp(3))
    product(1, 0)
    product(1, 1)
    for c in range(2):
        to("wb1", B, c, 0, w.at[1, one, c, yo], rlb.at[c, 0], yp(1))
        to("wb1", B, c, 2, w.at[1, one, c, yl], rb1.at[c, 1, one], yp(3))
    product(1, 2)
    product(1, 3)
    for c in range(2):
        to("wb1", B, c, 1, w.at[1, two, c, yo], rlb.at[c, 1], yp(3))
        to("wb1", B, c, 3, w.at[1, two, c, yr], rb1.at[c, 0, two], yp(1))
    for copy in gp:
        copy.wait_recv()
    mine = grows(128 * core + 32 * y + 8 * x, 8)
    total = gpart[mine, :]
    for n in plane:
        total = total + grx[n]
    grz[z] = total
    gz = [send(grz.at[z], grz.at[z], "gz", d - 1, zp(d)) for d in range(1, NZ)]

    product(0, xr)
    for c in range(2):
        to("wa1", A, c, 3, w.at[0, xr, c, low], ra1.at[c, 0, low], xp(1))
    product(0, xl)
    for c in range(2):
        to("wa1", A, c, 2, w.at[0, xl, c, top], ra1.at[c, 1, top], xp(3))

    def relay_a(c):
        taken("wa1", A, c, (0, 1))
        w[0, xr, c, top] = w[0, xr, c, top] + rla[c, 0]
        to("wa1", A, c, 4, w.at[0, xr, c, top], ra1.at[c, 0, top], xp(1))
        w[0, xl, c, low] = w[0, xl, c, low] + rla[c, 1]
        to("wa1", A, c, 5, w.at[0, xl, c, low], ra1.at[c, 1, low], xp(3))

    def relay_b(c):
        taken("wb1", B, c, (0, 1))
        w[1, one, c, yr] = w[1, one, c, yr] + rlb[c, 0]
        to("wb1", B, c, 4, w.at[1, one, c, yr], rb1.at[c, 0, one], yp(1))
        w[1, two, c, yl] = w[1, two, c, yl] + rlb[c, 1]
        to("wb1", B, c, 5, w.at[1, two, c, yl], rb1.at[c, 1, two], yp(3))

    for copy in gz:
        copy.wait_recv()
    total = grz[0]
    for k in range(1, NZ):
        total = total + grz[k]
    gram[mine, :] = total
    part = gram.at[mine]
    gp2 = [send(part, part, "gp2", n, pp(n)) for n in plane]
    relay_a(0)
    relay_b(0)
    product(0, x)
    relay_a(1)
    relay_b(1)

    def one_sum(c):
        taken("wa1", A, c, (2, 3, 4, 5))
        sa1[c] = w[0, x, c] + ra1[c, 0] + ra1[c, 1]
        for d in range(1, NY):
            part = sa1.at[c, yrows(lax.rem(y + d, NY))]
            to("wa2", A, c, d - 1, part, ra2.at[c, d - 1], yp(d))
        taken("wb1", B, c, (2, 3, 4, 5))
        for g in range(NX):
            sb1[c, g] = w[1, g, c, me] + rb1[c, 0, g] + rb1[c, 1, g]
        for d in range(1, NX):
            to("wb2", B, c, d - 1, sb1.at[c, lax.rem(x + d, NX)], rb2.at[c, d - 1], xp(d))

    def two_sum(c):
        taken("wa2", A, c, range(3))
        s2[c, 0] = sa1[c, me] + ra2[c, 0] + ra2[c, 1] + ra2[c, 2]
        taken("wb2", B, c, range(3))
        s2[c, 1] = sb1[c, x] + rb2[c, 0] + rb2[c, 1] + rb2[c, 2]
        for d in range(1, NZ):
            part = s2.at[c, :, zrows(lax.rem(z + d, NZ))]
            to("w3", A, c, d - 1, part, r3.at[c, d - 1], zp(d))

    def three_sum(c):
        taken("w3", A, c, range(7))
        total = s2[c, :, zrows(z)]
        for k in range(NZ - 1):
            total = total + r3[c, k]
        mine = pl.ds(pl.multiple_of(y * 64 + z * 8, 8), 8)
        wf[:, x, c, mine] = total
        part = wf.at[:, x, c, mine]
        for d in range(1, NZ):
            to("wz", A, c, d - 1, part, part, zp(d))

    def four_spread(c):
        taken("wz", A, c, range(7))
        for d in range(1, NY):
            to("wa5", A, c, d - 1, wf.at[0, x, c, me], wf.at[0, x, c, me], yp(d))
        for d in range(1, NX):
            to("wb5", B, c, d - 1, wf.at[1, x, c, me], wf.at[1, x, c, me], xp(d))

    def spread(name, store, c, n, part, dev):
        to(name, store, c, n, part, part, dev)

    def five_spread(c):
        taken("wa5", A, c, range(3))
        spread("wa6", A, c, 0, wf.at[0, x, c, top], xp(1))
        spread("wa6", A, c, 1, wf.at[0, x, c, low], xp(3))
        spread("wa6", A, c, 2, wf.at[0, x, c, low], xp(1))
        spread("wa6", A, c, 3, wf.at[0, x, c, top], xp(3))
        taken("wb5", B, c, range(3))
        spread("wb6", B, c, 0, wf.at[1, one, c, me], yp(1))
        spread("wb6", B, c, 1, wf.at[1, two, c, me], yp(3))
        spread("wb6", B, c, 2, wf.at[1, two, c, me], yp(1))
        spread("wb6", B, c, 3, wf.at[1, one, c, me], yp(3))

    def six_pass(c):
        taken("wa6", A, c, (0, 1))
        spread("wa6", A, c, 4, wf.at[0, xl, c, top], xp(1))
        spread("wa6", A, c, 5, wf.at[0, xr, c, low], xp(3))
        taken("wb6", B, c, (0, 1))
        spread("wb6", B, c, 4, wf.at[1, one, c, yl], yp(1))
        spread("wb6", B, c, 5, wf.at[1, two, c, yr], yp(3))

    one_sum(0)
    for copy in gp2:
        copy.wait_recv()
    for copy in gp2:
        copy.wait_send()
    sent[:] = [copy for copy in sent if not any(copy is c for c in gp2)]
    rows = lax.broadcasted_iota(jnp.int32, (RANK, RANK), 0)
    cols = lax.broadcasted_iota(jnp.int32, (RANK, RANK), 1)
    linv[...] = jnp.where(rows == cols, 1.0, 0.0)
    parts = cholesky(gram, linv)

    def work(step):
        for _ in range(SCHEDULE[step]):
            next(parts, None)

    work(0)
    one_sum(1)
    two_sum(0)
    work(1)
    two_sum(1)
    three_sum(0)
    work(2)
    three_sum(1)
    four_spread(0)
    work(3)
    four_spread(1)
    five_spread(0)
    work(4)
    five_spread(1)
    six_pass(0)
    work(5)
    six_pass(1)

    for _ in parts:
        pass
    li = split(linv[...])
    ortho_out[...] = dot3(split(left[...]), li, NT)
    li = split(linv[...] * 0.25)
    for c in range(2):
        taken("wa6", A, c, (2, 3, 4, 5))
        taken("wb6", B, c, (2, 3, 4, 5))

    nown[...] = jnp.zeros_like(nown)
    for h in range(2):

        @pl.loop(0, NX)
        def _(g):
            part = jnp.concatenate([wf[h, g, 0], wf[h, g, 1]], axis=1)
            part = dot3(li, split(part), NN)
            right_out[:, pl.ds(pl.multiple_of(h * HALF + g * CH, CH), CH)] = part
            sq = part * part
            nown[...] += sq[:, :128] + sq[:, 128:]

    ns = send(nown, nrec, "n", 0, cp)
    ns.wait_recv()
    norms = jnp.sqrt(jnp.sum(nown[...] + nrec[...], axis=1, keepdims=True) + 1e-06)
    norm_out[...] = jnp.broadcast_to(norms, (RANK, 128))
    mine = pl.ds(pl.multiple_of(f * 8, 8), 8)
    newb_out[...] = right_out[mine, :] / norm_out[mine, 0:1]

    for copy in sent:
        copy.wait_send()


def factors(momentum, grad, basis_t):
    v = pltpu.VMEM
    any_ = pl.BlockSpec(memory_space=pltpu.HBM)
    vm = pl.BlockSpec(memory_space=pltpu.VMEM)
    return pl.pallas_call(
        kernel,
        out_shape=(
            jax.ShapeDtypeStruct((RANK, NB), F32),
            jax.ShapeDtypeStruct((MB, RANK), F32),
            jax.ShapeDtypeStruct((RANK, 128), F32),
            jax.ShapeDtypeStruct((8, NB), F32),
        ),
        in_specs=[any_, any_, vm],
        out_specs=(vm, vm, vm, vm),
        scratch_shapes=[
            v((MB, NB), F32), v((MB, NB), BF16), v((MB, NB), BF16), v((MB, NB), BF16),
            v((2, NX, NZ, 8, HALF), F32),
            v((MB, RANK), F32), v((MB // 2, RANK), F32), v((3, MB // 8, RANK), F32),
            v((MB, RANK), F32), v((RANK, MB // 2), BF16), v((RANK, MB // 2), BF16),
            v((RANK, RANK), F32), v((32, 8, RANK), F32), v((NZ, 8, RANK), F32),
            v((RANK, RANK), F32), v((RANK, RANK), F32),
            v((2, NX, 2, RANK, LN), F32),
            v((2, 2, RANK // 2, LN), F32), v((2, 2, NX // 2, 64, LN), F32),
            v((2, 2, RANK, LN), F32), v((2, 2, NX, 64, LN), F32),
            v((2, RANK, LN), F32), v((2, NX, 64, LN), F32),
            v((2, 3, 64, LN), F32), v((2, 3, 64, LN), F32), v((2, 2, 64, LN), F32),
            v((2, 7, 2, 8, LN), F32), v((2, NX, 2, RANK, LN), F32),
            v((RANK, 128), F32), v((RANK, 128), F32),
            pltpu.SemaphoreType.DMA((2,)),
            pltpu.SemaphoreType.DMA((TOTAL,)),
            pltpu.SemaphoreType.DMA((TOTAL,)),
        ],
        compiler_params=pltpu.CompilerParams(
            collective_id=0, has_side_effects=True, vmem_limit_bytes=48 * 1024 * 1024
        ),
        name="factors",
    )(momentum, grad, basis_t)


def update_kernel(ortho, right, norm, mom, grad, weight, new_mom, new_w, ohi, olo):
    @pl.when(pl.program_id(0) == 0)
    def _():
        ohi[...], olo[...] = split(ortho[...])

    scale = 0.1 * math.sqrt(ROWS / COLS)
    part = right[...]
    buffer = mom[...] + grad[...].astype(F32)
    step = jnp.dot(ohi[...], part.astype(BF16), preferred_element_type=F32)
    new_mom[...] = buffer - 0.05 * step
    delta = dot3((ohi[...], olo[...]), split(part / norm[:, 0:1]), NN)
    new_w[...] = (weight[...].astype(F32) - scale * delta).astype(BF16)


def update(ortho, right, norm, momentum, grad, weight):
    cols = pl.BlockSpec((MB, CH), lambda i: (0, i))
    return pl.pallas_call(
        update_kernel,
        grid=(NB // CH,),
        out_shape=(
            jax.ShapeDtypeStruct((MB, NB), F32),
            jax.ShapeDtypeStruct((MB, NB), jnp.bfloat16),
        ),
        in_specs=[
            pl.BlockSpec((MB, RANK), lambda i: (0, 0)),
            pl.BlockSpec((RANK, CH), lambda i: (0, i)),
            pl.BlockSpec((RANK, 128), lambda i: (0, 0)),
            cols, cols, cols,
        ],
        out_specs=(cols, cols),
        scratch_shapes=[pltpu.VMEM((MB, RANK), BF16), pltpu.VMEM((MB, RANK), BF16)],
        compiler_params=pltpu.CompilerParams(vmem_limit_bytes=32 * 1024 * 1024),
        name="update",
    )(ortho, right, norm, momentum, grad, weight)


def body(weight, momentum, grad, basis):
    right, ortho, norm, new_basis_t = factors(momentum[0], grad[0], basis.T)
    new_momentum, new_weight = update(ortho, right, norm, momentum[0], grad[0], weight)
    return new_weight, new_momentum[None], new_basis_t.T


def solution(mesh):
    return jax.shard_map(
        body,
        mesh=mesh,
        in_specs=(
            P("fsdp", "tensor"),
            P("replica", "fsdp", "tensor"),
            P("replica", "fsdp", "tensor"),
            P("tensor", "fsdp"),
        ),
        out_specs=(P("fsdp", "tensor"), P("replica", "fsdp", "tensor"), P("tensor", "fsdp")),
        check_vma=False,
    )
```

time: 134 us -> 113 us (0.84)
  Pallas kernels: 130 us -> 109 us
    pallas_call x1, Pallas kernels: 120 us -> 103 us  [factors(): pl.pallas_call(kernel, out_shape=(jax.ShapeDtypeStruct((RANK, NB), F32),...]
    pallas_call x1, Pallas kernels: 10 us -> 5.88 us  [update(): pl.pallas_call(update_kernel, grid=(NB // CH,), out_shape=(jax.ShapeDtype...]
where the time goes in v2:
time: 113 us
  Pallas kernels  109 us (96%)
  local copies, waits for them, and re-layouts  2.97 us (3%)
    pallas_call x1, Pallas kernels, factors(): pl.pallas_call(kernel, out_shape=(jax.ShapeDtypeStruct((RANK, NB), F32),...  103 us
    pallas_call x1, Pallas kernels, update(): pl.pallas_call(update_kernel, grid=(NB // CH,), out_shape=(jax.ShapeDtype...  5.88 us
    unnamed x9, local copies, waits for them, and re-layouts  2.97 us

profile of v2, /device:TPU:1, one launch (start us, length us, event | category | flops | bytes accessed | tf_op | source)
XLA Modules:
  0.0 113.0 jit_solution(9471497856373257266)
XLA Ops:
  0.6 0.0 copy-start.1
  0.6 1.5 %copy-done.1 = bf16[1,448,2048]{2,1,0:T(8,128)(2,1)S(1)} copy-done((bf16[1,448,2048]{2,1,0:T(8,128)(2,1)S(1)}, bf16[1,448,2048]{2,1,0:T(8,128)(2,1)}, u32[]{:S(2)}) %copy-start.1) | copy-done | bytes 1835032
  2.1 0.0 copy-start.3
  2.1 0.8 copy-done.3
  3.0 0.0 copy-start
  3.0 0.0 copy-start.2
  3.0 103.5 %factors.1 = (f32[256,2048]{1,0:T(8,128)S(1)}, f32[448,256]{1,0:T(8,128)S(1)}, f32[256,128]{1,0:T(8,128)S(1)}, f32[8,2048]{1,0:T(8,128)S(1)}) custom-call(f32[448,2048]{1,0:T(8,128)} %bitcast.5, bf16[448,2048]{1,0:T(8,128)(2,1)S(1)} %bitcast.7, f32[8,2048]{1,0:T(8,128)S(1)} %bitcast.9), custom_call_target="tpu_custom_call" | custom-call | tf_op jit(solution)/shard_map/factors/pallas_call | solution.py:500
  106.4 0.0 copy-done
  106.5 0.0 copy-done.2
  106.5 5.9 %update.1 = (f32[448,2048]{1,0:T(8,128)}, bf16[448,2048]{1,0:T(8,128)(2,1)}) custom-call(f32[448,256]{1,0:T(8,128)S(1)} %get-tuple-element.9.ortho, f32[256,2048]{1,0:T(8,128)S(1)} %get-tuple-element.10.right, f32[256,128]{1,0:T(8,128)S(1)} %get-tuple-element.11.norm, f32[448,2048]{1,0:T(8,128)S(1)} %bitcast.6, bf16[448,2048]{1,0:T(8,128)(2,1)S(1)} %bitcast.8, ...), custom_call_target="tpu_custom_call" | custom-call | tf_op jit(solution)/shard_map/update/pallas_call | solution.py:551
  112.3 0.6 copy.8
Async XLA Ops:
  0.6 1.5 %copy-start.1 = (bf16[1,448,2048]{2,1,0:T(8,128)(2,1)S(1)}, bf16[1,448,2048]{2,1,0:T(8,128)(2,1)}, u32[]{:S(2)}) copy-start(bf16[1,448,2048]{2,1,0:T(8,128)(2,1)} %param.6) | copy-start | bytes 5505028
  2.1 0.8 copy-start.3
  3.0 103.5 %copy-start = (f32[1,448,2048]{2,1,0:T(8,128)S(1)}, f32[1,448,2048]{2,1,0:T(8,128)}, u32[]{:S(2)}) copy-start(f32[1,448,2048]{2,1,0:T(8,128)} %param.5) | copy-start | bytes 11010052
  3.0 103.5 %copy-start.2 = (bf16[448,2048]{1,0:T(8,128)(2,1)S(1)}, bf16[448,2048]{1,0:T(8,128)(2,1)}, u32[]{:S(2)}) copy-start(bf16[448,2048]{1,0:T(8,128)(2,1)} %weight.1) | copy-start | bytes 5505028

commit v3 on v2

--- a/solution.py
+++ b/solution.py
@@ -26,7 +26,7 @@
 COUNT, COUNTS = {}, {}
 TOTAL = 0
 for _name, _n in (
-    ("ax", 3), ("az", 28), ("bz", 7), ("bx", 3),
+    ("ax", 3), ("az", 28), ("bz", 7), ("bx", 32),
     ("lc", 1), ("ly", 3), ("ly2", 3), ("lc2", 1),
     ("gp", 32), ("gz", 7), ("gp2", 32),
     ("wa1", 12), ("wb1", 12), ("wa2", 6), ("wb2", 6), ("w3", 14),
@@ -118,9 +118,9 @@
 
 
 def kernel(
-    mom_hbm, grad_hbm, bas_in,
-    right_out, ortho_out, norm_out, newb_out,
-    buf, gra, bhi, blo, bas, lpart, lrc, lry, left, thi, tlo, gpart, grx, grz, gram, linv,
+    mom_hbm, grad_hbm, bas_hbm,
+    rhi_out, rlo_out, ortho_out, norm_out, newb_out,
+    buf, gra, bas_in, right, bhi, blo, bas, lpart, lrc, lry, left, thi, tlo, gpart, grx, grz, gram, linv,
     w, rla, rlb, ra1, rb1, sa1, sb1, ra2, rb2, s2, r3, wf, nown, nrec,
     lsem, ssem, rsem,
 ):
@@ -142,6 +142,8 @@
 
     load_m = pltpu.make_async_copy(mom_hbm, buf, lsem.at[0])
     load_g = pltpu.make_async_copy(grad_hbm, gra, lsem.at[1])
+    load_b = pltpu.make_async_copy(bas_hbm, bas_in, lsem.at[2])
+    load_b.start()
     load_m.start()
     load_g.start()
 
@@ -159,9 +161,6 @@
         copy.start()
         sent.append(copy)
         return copy
-
-    bas[0, x, z] = bas_in[:, :HALF]
-    bas[1, x, z] = bas_in[:, HALF:]
 
     barrier = pltpu.get_barrier_semaphore()
     plane = {}
@@ -175,9 +174,12 @@
         px, py, pc = plane[n]
         return (py, px * NZ + z, pc)
 
-    peers = [zp(d) for d in range(1, NZ)] + [pp(n) for n in plane]
+    peers = [xp(d) for d in range(1, NX)] + [yp(d) for d in range(1, NY)] + [zp(1), zp(-1), cp]
     for dev in peers:
         pl.semaphore_signal(barrier, inc=1, device_id=dev, device_id_type=MESH)
+    load_b.wait()
+    bas[0, x, z] = bas_in[:, :HALF]
+    bas[1, x, z] = bas_in[:, HALF:]
     load_m.wait()
     load_g.wait()
 
@@ -194,29 +196,56 @@
         piece = bas.at[0, lax.rem(x - i + NX, NX), lax.rem(z - way * (step - 1) + NZ, NZ)]
         return send(piece, piece, "az", (16 if way < 0 else 0) + (step - 1) * 4 + i, zp(way))
 
+    def across(way, step):
+        n = step + (3 if way < 0 else 0)
+        piece = bas.at[1, x, lax.rem(z - way * step + NZ, NZ)]
+        for k, d in ((0, 1), (1, 3)):
+            hops["bx", n, k] = send(piece, piece, "bx", 4 * n + k, xp(d))
+
+    def pass_on(way, step):
+        n = step + (3 if way < 0 else 0)
+        at = lax.rem(z - way * step + NZ, NZ)
+        for k, d, src in ((0, 1, lax.rem(x + 3, NX)), (1, 3, lax.rem(x + 1, NX))):
+            hops.pop(("bx", n, k)).wait_recv()
+            piece = bas.at[1, src, at, :, k * 512 : k * 512 + 512]
+            hops["bx", n, k + 2] = send(piece, piece, "bx", 4 * n + k + 2, xp(d))
+
+    def ring_b(way, step):
+        piece = bas.at[1, x, lax.rem(z - way * (step - 1) + NZ, NZ)]
+        n = step - 1 + (3 if way < 0 else 0)
+        hops["bz", way, step] = send(piece, piece, "bz", n, zp(way))
+
     hops = {}
     mine = bas.at[0, x, z]
     ax = [send(mine, mine, "ax", d - 1, xp(d)) for d in range(1, NX)]
     hops[1, 1, 0] = ring(1, 1, 0)
     hops[-1, 1, 0] = ring(-1, 1, 0)
-    mine = bas.at[1, x, z]
-    bz = [send(mine, mine, "bz", d - 1, zp(d)) for d in range(1, NZ)]
+    ring_b(1, 1)
+    ring_b(-1, 1)
+    across(1, 0)
     for i in range(1, NX):
         ax[i - 1].wait_recv()
         hops[1, 1, i] = ring(1, 1, i)
         hops[-1, 1, i] = ring(-1, 1, i)
-    for copy in bz:
-        copy.wait_recv()
-    mine = bas.at[1, x]
-    bx = [send(mine, mine, "bx", d - 1, xp(d)) for d in range(1, NX)]
-    for step in range(2, 5):
+    for step in range(1, 5):
+        for way in (-1, 1):
+            if ("bz", way, step) in hops:
+                hops.pop(("bz", way, step)).wait_recv()
+                if step < (3 if way == 1 else 4):
+                    ring_b(way, step + 1)
+                across(way, step)
         for i in range(NX):
             for way in (1, -1):
-                if (way, step - 1, i) in hops:
-                    hops.pop((way, step - 1, i)).wait_recv()
-                if way == 1 or step < 4:
-                    hops[way, step, i] = ring(way, step, i)
-    for copy in list(hops.values()) + bx:
+                if (way, step, i) in hops and step < (4 if way == 1 else 3):
+                    hops.pop((way, step, i)).wait_recv()
+                    hops[way, step + 1, i] = ring(way, step + 1, i)
+        if step == 1:
+            pass_on(1, 0)
+        else:
+            pass_on(1, step - 1)
+            pass_on(-1, step - 1)
+    pass_on(-1, 4)
+    for copy in hops.values():
         copy.wait_recv()
 
     hm, qm = MB // 2, MB // 8
@@ -467,27 +496,42 @@
     li = split(linv[...])
     ortho_out[...] = dot3(split(left[...]), li, NT)
     li = split(linv[...] * 0.25)
-    for c in range(2):
-        taken("wa6", A, c, (2, 3, 4, 5))
+    nown[...] = jnp.zeros_like(nown)
+
+    def right_part(h, g):
+        part = jnp.concatenate([wf[h, g, 0], wf[h, g, 1]], axis=1)
+        part = dot3(li, split(part), NN)
+        cols = pl.ds(pl.multiple_of(h * HALF + g * CH, CH), CH)
+        right[:, cols] = part
+        hi, lo = split(part)
+        rhi_out[:, cols] = hi
+        rlo_out[:, cols] = lo
+        sq = part * part
+        nown[...] += sq[:, :128] + sq[:, 128:]
+
+    right_part(0, x)
+    for c in range(2):
+        taken("wa6", A, c, (2, 3))
+    right_part(0, xl)
+    right_part(0, xr)
+    for c in range(2):
+        taken("wa6", A, c, (4, 5))
+    right_part(0, xo)
+    for c in range(2):
         taken("wb6", B, c, (2, 3, 4, 5))
-
-    nown[...] = jnp.zeros_like(nown)
-    for h in range(2):
-
-        @pl.loop(0, NX)
-        def _(g):
-            part = jnp.concatenate([wf[h, g, 0], wf[h, g, 1]], axis=1)
-            part = dot3(li, split(part), NN)
-            right_out[:, pl.ds(pl.multiple_of(h * HALF + g * CH, CH), CH)] = part
-            sq = part * part
-            nown[...] += sq[:, :128] + sq[:, 128:]
+    for g in range(NX):
+        right_part(1, g)
 
     ns = send(nown, nrec, "n", 0, cp)
     ns.wait_recv()
+    ns.wait_send()
+    sent.pop()
     norms = jnp.sqrt(jnp.sum(nown[...] + nrec[...], axis=1, keepdims=True) + 1e-06)
-    norm_out[...] = jnp.broadcast_to(norms, (RANK, 128))
+    norms = jnp.broadcast_to(norms, (RANK, 128))
+    nown[...] = norms
+    norm_out[...] = norms.T[:8]
     mine = pl.ds(pl.multiple_of(f * 8, 8), 8)
-    newb_out[...] = right_out[mine, :] / norm_out[mine, 0:1]
+    newb_out[...] = right[mine, :] / nown[mine, 0:1]
 
     for copy in sent:
         copy.wait_send()
@@ -500,15 +544,17 @@
     return pl.pallas_call(
         kernel,
         out_shape=(
-            jax.ShapeDtypeStruct((RANK, NB), F32),
+            jax.ShapeDtypeStruct((RANK, NB), BF16),
+            jax.ShapeDtypeStruct((RANK, NB), BF16),
             jax.ShapeDtypeStruct((MB, RANK), F32),
-            jax.ShapeDtypeStruct((RANK, 128), F32),
+            jax.ShapeDtypeStruct((8, RANK), F32),
             jax.ShapeDtypeStruct((8, NB), F32),
         ),
-        in_specs=[any_, any_, vm],
-        out_specs=(vm, vm, vm, vm),
+        in_specs=[any_, any_, any_],
+        out_specs=(vm,) * 5,
         scratch_shapes=[
-            v((MB, NB), F32), v((MB, NB), BF16), v((MB, NB), BF16), v((MB, NB), BF16),
+            v((MB, NB), F32), v((MB, NB), BF16), v((8, NB), F32), v((RANK, NB), F32),
+            v((MB, NB), BF16), v((MB, NB), BF16),
             v((2, NX, NZ, 8, HALF), F32),
             v((MB, RANK), F32), v((MB // 2, RANK), F32), v((3, MB // 8, RANK), F32),
             v((MB, RANK), F32), v((RANK, MB // 2), BF16), v((RANK, MB // 2), BF16),
@@ -521,7 +567,7 @@
             v((2, 3, 64, LN), F32), v((2, 3, 64, LN), F32), v((2, 2, 64, LN), F32),
             v((2, 7, 2, 8, LN), F32), v((2, NX, 2, RANK, LN), F32),
             v((RANK, 128), F32), v((RANK, 128), F32),
-            pltpu.SemaphoreType.DMA((2,)),
+            pltpu.SemaphoreType.DMA((3,)),
             pltpu.SemaphoreType.DMA((TOTAL,)),
             pltpu.SemaphoreType.DMA((TOTAL,)),
         ],
@@ -532,45 +578,54 @@
     )(momentum, grad, basis_t)
 
 
-def update_kernel(ortho, right, norm, mom, grad, weight, new_mom, new_w, ohi, olo):
-    @pl.when(pl.program_id(0) == 0)
-    def _():
-        ohi[...], olo[...] = split(ortho[...])
-
+def update_kernel(ortho, rhi, rlo, norm, mom, grad, weight, mom_hbm, w_hbm, lhs, mom_v, w_v, sems):
+    lhs[:MB], _ = split(ortho[...])
+    hi, lo = split(ortho[...] / norm[0:1, :])
+    lhs[MB : 2 * MB] = hi
+    lhs[2 * MB :] = lo
     scale = 0.1 * math.sqrt(ROWS / COLS)
-    part = right[...]
-    buffer = mom[...] + grad[...].astype(F32)
-    step = jnp.dot(ohi[...], part.astype(BF16), preferred_element_type=F32)
-    new_mom[...] = buffer - 0.05 * step
-    delta = dot3((ohi[...], olo[...]), split(part / norm[:, 0:1]), NN)
-    new_w[...] = (weight[...].astype(F32) - scale * delta).astype(BF16)
-
-
-def update(ortho, right, norm, momentum, grad, weight):
-    cols = pl.BlockSpec((MB, CH), lambda i: (0, i))
+    copies = []
+    for n in range(NB // CH):
+        cols = slice(n * CH, n * CH + CH)
+        both = jnp.dot(lhs[...], rhi[:, cols], preferred_element_type=F32)
+        mom_v[n] = mom[:, cols] + grad[:, cols].astype(F32) - 0.05 * both[:MB]
+        copies.append(pltpu.make_async_copy(mom_v.at[n], mom_hbm.at[:, cols], sems.at[2 * n]))
+        copies[-1].start()
+        rest = jnp.dot(lhs[MB : 2 * MB], rlo[:, cols], preferred_element_type=F32)
+        delta = both[MB : 2 * MB] + (both[2 * MB :] + rest)
+        w_v[n] = (weight[:, cols].astype(F32) - scale * delta).astype(BF16)
+        copies.append(pltpu.make_async_copy(w_v.at[n], w_hbm.at[:, cols], sems.at[2 * n + 1]))
+        copies[-1].start()
+    for copy in copies:
+        copy.wait()
+
+
+def update(ortho, rhi, rlo, norm, momentum, grad, weight):
+    vm = pl.BlockSpec(memory_space=pltpu.VMEM)
+    any_ = pl.BlockSpec(memory_space=pltpu.HBM)
+    steps = NB // CH
     return pl.pallas_call(
         update_kernel,
-        grid=(NB // CH,),
         out_shape=(
             jax.ShapeDtypeStruct((MB, NB), F32),
-            jax.ShapeDtypeStruct((MB, NB), jnp.bfloat16),
+            jax.ShapeDtypeStruct((MB, NB), BF16),
         ),
-        in_specs=[
-            pl.BlockSpec((MB, RANK), lambda i: (0, 0)),
-            pl.BlockSpec((RANK, CH), lambda i: (0, i)),
-            pl.BlockSpec((RANK, 128), lambda i: (0, 0)),
-            cols, cols, cols,
+        in_specs=[vm] * 7,
+        out_specs=(any_, any_),
+        scratch_shapes=[
+            pltpu.VMEM((3 * MB, RANK), BF16),
+            pltpu.VMEM((steps, MB, CH), F32),
+            pltpu.VMEM((steps, MB, CH), BF16),
+            pltpu.SemaphoreType.DMA((2 * steps,)),
         ],
-        out_specs=(cols, cols),
-        scratch_shapes=[pltpu.VMEM((MB, RANK), BF16), pltpu.VMEM((MB, RANK), BF16)],
         compiler_params=pltpu.CompilerParams(vmem_limit_bytes=32 * 1024 * 1024),
         name="update",
-    )(ortho, right, norm, momentum, grad, weight)
+    )(ortho, rhi, rlo, norm, momentum, grad, weight)
 
 
 def body(weight, momentum, grad, basis):
-    right, ortho, norm, new_basis_t = factors(momentum[0], grad[0], basis.T)
-    new_momentum, new_weight = update(ortho, right, norm, momentum[0], grad[0], weight)
+    rhi, rlo, ortho, norm, new_basis_t = factors(momentum[0], grad[0], basis.T)
+    new_momentum, new_weight = update(ortho, rhi, rlo, norm, momentum[0], grad[0], weight)
     return new_weight, new_momentum[None], new_basis_t.T
 
 

time: 113 us -> 109 us (0.965)
  Pallas kernels: 109 us -> 105 us
    pallas_call x2, Pallas kernels: 109 us -> 105 us  [the longest x1 102 us: factors(): pl.pallas_call(kernel, out_shape=(jax.ShapeDtypeStruct((RANK, NB), BF16),...]
where the time goes in v3:
time: 109 us
  Pallas kernels  105 us (96%)
  local copies, waits for them, and re-layouts  2.97 us (3%)
    pallas_call x1, Pallas kernels, factors(): pl.pallas_call(kernel, out_shape=(jax.ShapeDtypeStruct((RANK, NB), BF16),...  102 us
    pallas_call x1, Pallas kernels, update(): pl.pallas_call(update_kernel, out_shape=(jax.ShapeDtypeStruct((MB, NB), F...  3.54 us
    unnamed x9, local copies, waits for them, and re-layouts  2.97 us

profile of v3, /device:TPU:1, one launch (start us, length us, event | category | flops | bytes accessed | tf_op | source)
XLA Modules:
  0.0 109.0 jit_solution(7252818627932385499)
XLA Ops:
  0.6 0.0 copy-start.1
  0.6 1.5 %copy-done.1 = bf16[1,448,2048]{2,1,0:T(8,128)(2,1)S(1)} copy-done((bf16[1,448,2048]{2,1,0:T(8,128)(2,1)S(1)}, bf16[1,448,2048]{2,1,0:T(8,128)(2,1)}, u32[]{:S(2)}) %copy-start.1) | copy-done | bytes 1835032
  2.1 0.0 copy-start.3
  2.1 0.8 copy-done.3
  3.0 0.0 copy-start
  3.0 0.0 copy-start.2
  3.0 101.9 %factors.1 = (bf16[256,2048]{1,0:T(8,128)(2,1)S(1)}, bf16[256,2048]{1,0:T(8,128)(2,1)S(1)}, f32[448,256]{1,0:T(8,128)S(1)}, f32[8,256]{1,0:T(8,128)S(1)}, f32[8,2048]{1,0:T(8,128)S(1)}) custom-call(f32[448,2048]{1,0:T(8,128)} %bitcast.5, bf16[448,2048]{1,0:T(8,128)(2,1)S(1)} %bitcast.7, f32[8,2048]{1,0:T(8,128)S(1)} %bitcast.9), custom_call_target="tpu_custom_call" | custom-call | tf_op jit(solution)/shard_map/factors/pallas_call | solution.py:544
  104.8 0.0 copy-done
  104.8 0.0 copy-done.2
  104.9 3.5 %update.1 = (f32[448,2048]{1,0:T(8,128)}, bf16[448,2048]{1,0:T(8,128)(2,1)}) custom-call(f32[448,256]{1,0:T(8,128)S(1)} %get-tuple-element.10.ortho, bf16[256,2048]{1,0:T(8,128)(2,1)S(1)} %get-tuple-element.11.rhi, bf16[256,2048]{1,0:T(8,128)(2,1)S(1)} %get-tuple-element.12.rlo, f32[8,256]{1,0:T(8,128)S(1)} %get-tuple-element.13.norm, ...), custom_call_target="tpu_custom_call" | custom-call | tf_op jit(solution)/shard_map/update/pallas_call | solution.py:607
  108.4 0.6 copy.8
Async XLA Ops:
  0.6 1.5 %copy-start.1 = (bf16[1,448,2048]{2,1,0:T(8,128)(2,1)S(1)}, bf16[1,448,2048]{2,1,0:T(8,128)(2,1)}, u32[]{:S(2)}) copy-start(bf16[1,448,2048]{2,1,0:T(8,128)(2,1)} %param.6) | copy-start | bytes 5505028
  2.1 0.8 copy-start.3
  3.0 101.9 %copy-start = (f32[1,448,2048]{2,1,0:T(8,128)S(1)}, f32[1,448,2048]{2,1,0:T(8,128)}, u32[]{:S(2)}) copy-start(f32[1,448,2048]{2,1,0:T(8,128)} %param.5) | copy-start | bytes 11010052
  3.0 101.9 %copy-start.2 = (bf16[448,2048]{1,0:T(8,128)(2,1)S(1)}, bf16[448,2048]{1,0:T(8,128)(2,1)}, u32[]{:S(2)}) copy-start(bf16[448,2048]{1,0:T(8,128)(2,1)} %weight.1) | copy-start | bytes 5505028

commit v4 on v3

--- a/solution.py
+++ b/solution.py
@@ -578,13 +578,17 @@
     )(momentum, grad, basis_t)
 
 
-def update_kernel(ortho, rhi, rlo, norm, mom, grad, weight, mom_hbm, w_hbm, lhs, mom_v, w_v, sems):
+def update_kernel(
+    ortho, rhi, rlo, norm, newb, mom, grad, weight,
+    mom_hbm, w_hbm, newb_hbm, lhs, mom_v, w_v, sems,
+):
+    copies = [pltpu.make_async_copy(newb, newb_hbm, sems.at[2 * NB // CH])]
+    copies[0].start()
     lhs[:MB], _ = split(ortho[...])
     hi, lo = split(ortho[...] / norm[0:1, :])
     lhs[MB : 2 * MB] = hi
     lhs[2 * MB :] = lo
     scale = 0.1 * math.sqrt(ROWS / COLS)
-    copies = []
     for n in range(NB // CH):
         cols = slice(n * CH, n * CH + CH)
         both = jnp.dot(lhs[...], rhi[:, cols], preferred_element_type=F32)
@@ -600,7 +604,7 @@
         copy.wait()
 
 
-def update(ortho, rhi, rlo, norm, momentum, grad, weight):
+def update(ortho, rhi, rlo, norm, newb, momentum, grad, weight):
     vm = pl.BlockSpec(memory_space=pltpu.VMEM)
     any_ = pl.BlockSpec(memory_space=pltpu.HBM)
     steps = NB // CH
@@ -609,23 +613,26 @@
         out_shape=(
             jax.ShapeDtypeStruct((MB, NB), F32),
             jax.ShapeDtypeStruct((MB, NB), BF16),
+            jax.ShapeDtypeStruct((8, NB), F32),
         ),
-        in_specs=[vm] * 7,
-        out_specs=(any_, any_),
+        in_specs=[vm] * 8,
+        out_specs=(any_, any_, any_),
         scratch_shapes=[
             pltpu.VMEM((3 * MB, RANK), BF16),
             pltpu.VMEM((steps, MB, CH), F32),
             pltpu.VMEM((steps, MB, CH), BF16),
-            pltpu.SemaphoreType.DMA((2 * steps,)),
+            pltpu.SemaphoreType.DMA((2 * steps + 1,)),
         ],
         compiler_params=pltpu.CompilerParams(vmem_limit_bytes=32 * 1024 * 1024),
         name="update",
-    )(ortho, rhi, rlo, norm, momentum, grad, weight)
+    )(ortho, rhi, rlo, norm, newb, momentum, grad, weight)
 
 
 def body(weight, momentum, grad, basis):
-    rhi, rlo, ortho, norm, new_basis_t = factors(momentum[0], grad[0], basis.T)
-    new_momentum, new_weight = update(ortho, rhi, rlo, norm, momentum[0], grad[0], weight)
+    rhi, rlo, ortho, norm, newb = factors(momentum[0], grad[0], basis.T)
+    new_momentum, new_weight, new_basis_t = update(
+        ortho, rhi, rlo, norm, newb, momentum[0], grad[0], weight
+    )
     return new_weight, new_momentum[None], new_basis_t.T
 
 

time: 109 us -> 109 us (level)
    unnamed x9 -> x8, local copies, waits for them, and re-layouts: 2.97 us -> 2.34 us
where the time goes in v4:
time: 109 us
  Pallas kernels  105 us (96%)
  local copies, waits for them, and re-layouts  2.34 us (2%)
    pallas_call x1, Pallas kernels, factors(): pl.pallas_call(kernel, out_shape=(jax.ShapeDtypeStruct((RANK, NB), BF16),...  102 us
    pallas_call x1, Pallas kernels, update(): pl.pallas_call(update_kernel, out_shape=(jax.ShapeDtypeStruct((MB, NB), F...  3.54 us
    unnamed x8, local copies, waits for them, and re-layouts  2.34 us

profile of v4, /device:TPU:1, one launch (start us, length us, event | category | flops | bytes accessed | tf_op | source)
XLA Modules:
  0.0 108.6 jit_solution(7824613481637079929)
XLA Ops:
  0.6 0.0 copy-start.1
  0.6 1.5 %copy-done.1 = bf16[1,448,2048]{2,1,0:T(8,128)(2,1)S(1)} copy-done((bf16[1,448,2048]{2,1,0:T(8,128)(2,1)S(1)}, bf16[1,448,2048]{2,1,0:T(8,128)(2,1)}, u32[]{:S(2)}) %copy-start.1) | copy-done | bytes 1835032
  2.1 0.0 copy-start.3
  2.1 0.8 copy-done.3
  3.0 0.0 copy-start
  3.0 0.0 copy-start.2
  3.0 101.9 %factors.1 = (bf16[256,2048]{1,0:T(8,128)(2,1)S(1)}, bf16[256,2048]{1,0:T(8,128)(2,1)S(1)}, f32[448,256]{1,0:T(8,128)S(1)}, f32[8,256]{1,0:T(8,128)S(1)}, f32[8,2048]{1,0:T(8,128)S(1)}) custom-call(f32[448,2048]{1,0:T(8,128)} %bitcast.5, bf16[448,2048]{1,0:T(8,128)(2,1)S(1)} %bitcast.7, f32[8,2048]{1,0:T(8,128)S(1)} %bitcast.9), custom_call_target="tpu_custom_call" | custom-call | tf_op jit(solution)/shard_map/factors/pallas_call | solution.py:544
  104.8 0.0 copy-done
  104.8 0.0 copy-done.2
  104.9 3.5 %update.1 = (f32[448,2048]{1,0:T(8,128)}, bf16[448,2048]{1,0:T(8,128)(2,1)}, f32[8,2048]{1,0:T(8,128)}) custom-call(f32[448,256]{1,0:T(8,128)S(1)} %get-tuple-element.11.ortho, bf16[256,2048]{1,0:T(8,128)(2,1)S(1)} %get-tuple-element.12.rhi, bf16[256,2048]{1,0:T(8,128)(2,1)S(1)} %get-tuple-element.13.rlo, f32[8,256]{1,0:T(8,128)S(1)} %get-tuple-element.14.norm, ...), custom_call_target="tpu_custom_call" | custom-call | tf_op jit(solution)/shard_map/update/pallas_call | solution.py:611
Async XLA Ops:
  0.6 1.5 %copy-start.1 = (bf16[1,448,2048]{2,1,0:T(8,128)(2,1)S(1)}, bf16[1,448,2048]{2,1,0:T(8,128)(2,1)}, u32[]{:S(2)}) copy-start(bf16[1,448,2048]{2,1,0:T(8,128)(2,1)} %param.6) | copy-start | bytes 5505028
  2.1 0.8 copy-start.3
  3.0 101.9 %copy-start = (f32[1,448,2048]{2,1,0:T(8,128)S(1)}, f32[1,448,2048]{2,1,0:T(8,128)}, u32[]{:S(2)}) copy-start(f32[1,448,2048]{2,1,0:T(8,128)} %param.5) | copy-start | bytes 11010052
  3.0 101.9 %copy-start.2 = (bf16[448,2048]{1,0:T(8,128)(2,1)S(1)}, bf16[448,2048]{1,0:T(8,128)(2,1)}, u32[]{:S(2)}) copy-start(bf16[448,2048]{1,0:T(8,128)(2,1)} %weight.1) | copy-start | bytes 5505028
